TPU v7x, 32 devices: a whole 2x2x4 slice. The times are simulated.
32 devices in a mesh: parts: 2 (over x), sta: 16 (over z, y, core).
Axes of the slice: x: 2, y: 2, z: 4, core: 2. Of those that a mesh axis runs over, the one named last changes fastest.
Arguments:
- data: bfloat16 [32, 3, 896], P(('parts', 'sta')), parts along dimension 0, may hold values from -40 to 40
- templates: bfloat16 [128, 3, 512], P('sta'), may hold values from -12 to 12
- station_lists: int32 [16, 128], replicated, may hold values from 0 to 15, as said below
- counts: int32 [128], replicated, may hold values from 8 to 16
- offsets: int32 [16, 128], replicated, may hold values from 0 to 127
Outputs:
- detection: float32 [256, 256], P(('parts', 'sta')), parts along dimension 0
There are 2 independent parts, one for each index of `parts`. A program takes and returns all parts, laid end to end along the dimension named above; an argument that names none is the same for every part. Nothing has to cross between parts.
Inputs may be any that keep to these rules, and one draw needn't show every extreme that they name: `station_lists`: each column names every one of the 16 stations once; template t uses the stations in entries k < counts[t] of its column. offsets[k, t] belongs to the station in entry k of template t's column.
All inputs are finite; a program needn't handle non-finite values.
Results may differ from a plain program's by a relative error of at most 0.0028.
Values may be sent and summed in bfloat16 or wider, within the bound.
A program may use at most 64 MiB of HBM per device.

v0:
```python
import functools

import jax
import jax.numpy as jnp
from jax import lax
from jax.experimental import pallas as pl
from jax.experimental.pallas import tpu as pltpu
from jax.sharding import PartitionSpec as P

NCH = 3
L = 512
NTAU = 256
LANES = 128
ROWS = 8
F32 = jnp.float32
MESH = pl.DeviceIdType.MESH


def network_kernel(
    n, data_hbm, templates_hbm, lists_hbm, counts_hbm, offsets_hbm, out_ref,
    templates_ref, lists_ref, counts_ref, offsets_ref,
    slots, staged, bands, factors_ref, fetch_sem, send_sem, recv_sem,
):
    me = lax.axis_index("sta")
    fetches = [
        pltpu.make_async_copy(source, target, fetch_sem.at[i])
        for i, (source, target) in enumerate(
            [
                (data_hbm.at[0], slots.at[me]), (templates_hbm, templates_ref), (lists_hbm, lists_ref),
                (counts_hbm, counts_ref), (offsets_hbm, offsets_ref),
            ]
        )
    ]
    fetches[0].start()
    fetches[1].start()
    samples_len = data_hbm.shape[2]
    blocks = samples_len // LANES
    lag_blocks = (samples_len - L) // LANES
    out_blocks = NTAU // LANES
    wave_blocks = L // LANES
    span = L + LANES
    own = templates_ref.shape[1]

    barrier = pltpu.get_barrier_semaphore()

    for step in range(1, n):
        pl.semaphore_signal(
            barrier, inc=1, device_id={"sta": lax.rem(me + step, n)}, device_id_type=MESH
        )

    row_id = lax.broadcasted_iota(jnp.int32, (LANES, LANES), 0)
    lane_id = lax.broadcasted_iota(jnp.int32, (LANES, LANES), 1)
    upper = lane_id >= row_id
    zeros = jnp.zeros((LANES, LANES), F32)

    def build():
        fetches[1].wait()
        for c in range(NCH):
            values = templates_ref[c].astype(F32)
            mean = jnp.sum(values, axis=1, keepdims=True) / L
            centered = (values - mean).astype(jnp.bfloat16).astype(F32)
            power = jnp.sum(centered * centered, axis=1, keepdims=True) / L
            factor = 1.0 / (NCH * L * jnp.sqrt(power + 1e-06))
            factors_ref[c] = jnp.broadcast_to(factor, (own, LANES))
            for t in range(own):
                before = zeros
                for k in range(wave_blocks + 1):
                    if k < wave_blocks:
                        row = centered[t : t + 1, LANES * k : LANES * (k + 1)]
                        turned = pltpu.roll(
                            jnp.broadcast_to(row, (LANES, LANES)), 0, 1, stride=1, stride_axis=0
                        )
                    else:
                        turned = zeros
                    bands[c, LANES * k : LANES * (k + 1), LANES * t : LANES * (t + 1)] = (
                        jnp.where(upper, turned, before).T.astype(jnp.bfloat16)
                    )
                    before = turned

    pl.when(me < n // 4)(build)

    pl.semaphore_wait(barrier, n - 1)

    def copy_to(step):
        return pltpu.make_async_remote_copy(
            src_ref=slots.at[me],
            dst_ref=slots.at[me],
            send_sem=send_sem.at[step],
            recv_sem=recv_sem.at[step],
            device_id={"sta": lax.rem(me + step, n)},
            device_id_type=MESH,
        )

    fetches[0].wait()
    for step in range(1, n):
        copy_to(step).start()
    for fetch in fetches[2:]:
        fetch.start()
    pl.when(me >= n // 4)(build)

    for fetch in fetches[2:]:
        fetch.wait()
    width = counts_ref.shape[1]
    station = lax.broadcasted_iota(jnp.int32, (n, width), 0)
    lane = lax.broadcasted_iota(jnp.int32, (n, width), 1)
    counts = counts_ref[...]
    table = jnp.zeros((n, width), jnp.int32)
    for k in range(lists_ref.shape[0]):
        match = (lists_ref[k : k + 1, :] == station) & (k < counts)
        table = table + jnp.where(match, offsets_ref[k : k + 1, :] + 256, 0)
    table = table.astype(F32)
    codes = [
        jnp.sum(jnp.where(lane == me * own + t, table, 0.0), axis=1, keepdims=True).astype(jnp.int32)
        for t in range(own)
    ]

    window_row = lax.broadcasted_iota(jnp.int32, (span, LANES), 0)
    window_lane = lax.broadcasted_iota(jnp.int32, (span, LANES), 1)
    window = ((window_row >= window_lane) & (window_row < window_lane + L)).astype(F32)
    window = window.astype(jnp.bfloat16)

    def stage(sender):
        samples = slots[sender].astype(F32)
        for b in range(blocks):
            first_row = pl.multiple_of(sender * (ROWS * blocks) + ROWS * b, ROWS)
            staged[pl.ds(first_row, NCH), :] = samples[:, LANES * b : LANES * (b + 1)]

    stage(me)

    @pl.loop(1, n)
    def receive(ahead):
        step = n - ahead
        sender = lax.rem(me + ahead, n)
        pltpu.make_async_remote_copy(
            src_ref=slots.at[sender],
            dst_ref=slots.at[sender],
            send_sem=send_sem.at[step],
            recv_sem=recv_sem.at[step],
            device_id={"sta": sender},
            device_id_type=MESH,
        ).wait_recv()
        stage(sender)

    def spread(parts):
        return jnp.concatenate(
            [
                jnp.concatenate(parts[b : b + wave_blocks + 1], axis=1)
                for b in range(lag_blocks)
            ],
            axis=0,
        )

    held = lag_blocks * n
    operands, squares = [], []
    for c in range(NCH):
        parts = [staged[pl.ds(ROWS * b + c, n, stride=ROWS * blocks), :] for b in range(blocks)]
        operands.append(spread([x.astype(jnp.bfloat16) for x in parts]))
        high = [(x * x).astype(jnp.bfloat16) for x in parts]
        low = [(x * x - h.astype(F32)).astype(jnp.bfloat16) for x, h in zip(parts, high)]
        squares.append((spread(high), spread(low)))
    fitted = [None] * own
    for c in range(NCH):
        stacked = jnp.concatenate([operands[c], *squares[c]], axis=0)
        sums = jnp.dot(stacked, window, preferred_element_type=F32)
        mean_one = sums[:held] / L
        mean_two = (sums[held : 2 * held] + sums[2 * held :]) / L
        inverse = 1.0 / jnp.sqrt(mean_two - mean_one * mean_one + 1e-05)
        products = jnp.dot(operands[c], bands[c], preferred_element_type=F32)
        for t in range(own):
            term = products[:, LANES * t : LANES * (t + 1)] * (inverse * factors_ref[c, t : t + 1, :])
            fitted[t] = term if c == 0 else fitted[t] + term

    lane = lax.broadcasted_iota(jnp.int32, (n, LANES), 1)
    for t in range(own):
        code = jnp.broadcast_to(codes[t], (n, LANES))
        shift = code & 127
        member = code >= 256
        turn = (lane + shift) & (LANES - 1)
        current = jnp.take_along_axis(
            fitted[t], jnp.concatenate([turn] * lag_blocks, axis=0), axis=1,
            mode="promise_in_bounds",
        )
        stays = lane + shift < LANES
        for b in range(out_blocks):
            picked = jnp.where(
                stays, current[n * b : n * (b + 1)], current[n * (b + 1) : n * (b + 2)]
            )
            out_ref[t : t + 1, LANES * b : LANES * (b + 1)] = jnp.sum(
                jnp.where(member, picked, 0.0), axis=0, keepdims=True
            )

    @pl.loop(1, n)
    def sent(step):
        copy_to(step).wait_send()


def body(n, data, templates, station_lists, counts, offsets):
    own, _, length = templates.shape
    operands = (data, jnp.transpose(templates, (1, 0, 2)), station_lists, counts[None, :], offsets)
    return pl.pallas_call(
        functools.partial(network_kernel, n),
        out_shape=jax.ShapeDtypeStruct((own, NTAU), F32),
        in_specs=[pl.BlockSpec(memory_space=pltpu.HBM)] * len(operands),
        out_specs=pl.BlockSpec(memory_space=pltpu.VMEM),
        scratch_shapes=[pltpu.VMEM(x.shape, x.dtype) for x in operands[1:]]
        + [
            pltpu.VMEM((n, *data.shape[1:]), data.dtype),
            pltpu.VMEM((n * ROWS * (data.shape[2] // LANES), LANES), F32),
            pltpu.VMEM((NCH, length + LANES, own * LANES), jnp.bfloat16),
            pltpu.VMEM((NCH, own, LANES), F32),
            pltpu.SemaphoreType.DMA((len(operands),)),
            pltpu.SemaphoreType.DMA((n,)),
            pltpu.SemaphoreType.DMA((n,)),
        ],
        compiler_params=pltpu.CompilerParams(
            collective_id=0, has_side_effects=True, vmem_limit_bytes=40 * 1024 * 1024
        ),
    )(*[pltpu.with_memory_space_constraint(x, pltpu.HBM) for x in operands])


def solution(mesh):
    placed = (P(("parts", "sta"), None, None), P("sta", None, None), P(), P(), P())
    return jax.shard_map(
        functools.partial(body, mesh.shape["sta"]), mesh=mesh, in_specs=placed,
        out_specs=P(("parts", "sta"), None), check_vma=False,
    )
```

profile of v0, /device:TPU:0, one launch (start us, length us, event | category | flops | bytes accessed | tf_op | source)
XLA Modules:
  0.0 11.0 jit_solution(13593243283863319665)
XLA Ops:
  0.0 10.4 %shard_map.55 = f32[8,256]{1,0:T(8,128)S(1)} custom-call(bf16[1,3,896]{2,1,0:T(4,128)(2,1)} %data_hbm.1, bf16[3,8,512]{2,1,0:T(8,128)(2,1)} %bitcast.2, s32[16,128]{1,0:T(8,128)} %lists_hbm.1, s32[1,128]{1,0:T(1,128)} %bitcast.3, s32[16,128]{1,0:T(8,128)} %offsets_hbm.1), custom_call_target="tpu_custom_call" | custom-call | tf_op jit(solution)/shard_map/pallas_call | solution.py:200
  10.4 0.6 %copy.7 = f32[8,256]{1,0:T(8,128)} copy(f32[8,256]{1,0:T(8,128)S(1)} %shard_map.55) | data formatting | bytes 16384
where the time goes:
time: 11.2 us; the launch traced here: 11 us
  Pallas kernels  10.4 us (93%)
  local copies, waits for them, and re-layouts  0.6 us (5%)
    pallas_call x1, Pallas kernels, body(): pl.pallas_call(functools.partial(network_kernel, n), out_shape=jax.ShapeD...  10.4 us
    unnamed x1, local copies, waits for them, and re-layouts  0.6 us

commit v1 on v0

v1 whole, which is shorter than its diff:
```python
import functools

import jax
import jax.numpy as jnp
from jax import lax
from jax.experimental import pallas as pl
from jax.experimental.pallas import tpu as pltpu
from jax.sharding import PartitionSpec as P

NCH = 3
L = 512
NTAU = 256
LANES = 128
ROWS = 8
LAGS = 32
SUB = LANES // LAGS
F32 = jnp.float32
BF16 = jnp.bfloat16
MESH = pl.DeviceIdType.MESH


def network_kernel(
    n, data_hbm, templates_hbm, lists_hbm, counts_hbm, offsets_hbm, out_ref,
    templates_ref, lists_ref, counts_ref, offsets_ref,
    slots, staged, bands, factors_ref, window_ref, lane_codes, sources,
    fetch_sem, send_sem, recv_sem, late_sem,
):
    me = lax.axis_index("sta")
    fetches = [
        pltpu.make_async_copy(source, target, fetch_sem.at[i])
        for i, (source, target) in enumerate(
            [
                (data_hbm.at[0], slots.at[me]), (templates_hbm, templates_ref), (lists_hbm, lists_ref),
                (counts_hbm, counts_ref), (offsets_hbm, offsets_ref),
            ]
        )
    ]
    fetches[0].start()
    samples_len = data_hbm.shape[2]
    blocks = samples_len // LANES
    lag_blocks = (samples_len - L) // LANES
    wave_blocks = L // LANES
    depth = L + LANES
    own = templates_ref.shape[1]
    groups = own // SUB
    station_rows = ROWS * blocks
    parts_of_lags = lag_blocks * SUB

    late_from = n - n // 4
    early = me < late_from
    barrier = pltpu.get_barrier_semaphore()

    def to_others(low, high, act):
        for d in range(low, high):
            pl.when(me != d)(functools.partial(act, d))

    def greet(d):
        pl.semaphore_signal(barrier, inc=1, device_id={"sta": jnp.int32(d)}, device_id_type=MESH)

    def announce(d):
        pl.semaphore_signal(late_sem, inc=1, device_id={"sta": jnp.int32(d)}, device_id_type=MESH)

    to_others(late_from, n, greet)

    @pl.when(early)
    def _():
        to_others(0, late_from, greet)

    for fetch in fetches[1:]:
        fetch.start()

    def copy_to(target):
        return pltpu.make_async_remote_copy(
            src_ref=slots.at[me],
            dst_ref=slots.at[me],
            send_sem=send_sem.at[target],
            recv_sem=recv_sem.at[me],
            device_id={"sta": target},
            device_id_type=MESH,
        )

    def send(d):
        copy_to(jnp.int32(d)).start()

    fetches[0].wait()

    @pl.when(early)
    def _():
        pl.semaphore_wait(barrier, late_from - 1)
        to_others(0, late_from, send)

    @pl.when(jnp.logical_not(early))
    def _():
        pl.semaphore_wait(barrier, n - 1)
        for d in range(late_from):
            announce(d)
        to_others(0, n, send)

    window_row = lax.broadcasted_iota(jnp.int32, (depth, LANES), 0)
    window_lane = lax.broadcasted_iota(jnp.int32, (depth, LANES), 1)
    window = ((window_row >= window_lane) & (window_row < window_lane + L)).astype(F32)
    window_ref[...] = window.astype(BF16)

    fetches[1].wait()
    band_row = lax.broadcasted_iota(jnp.int32, (LAGS, LANES), 0)
    band_lane = lax.broadcasted_iota(jnp.int32, (LAGS, LANES), 1)
    upper = band_lane >= band_row
    owner_row = lax.broadcasted_iota(jnp.int32, (own, own * LAGS), 0)
    owner_lane = lax.broadcasted_iota(jnp.int32, (own, own * LAGS), 1) // LAGS
    for c in range(NCH):
        values = templates_ref[c].astype(F32)
        mean = jnp.sum(values, axis=1, keepdims=True) / L
        centered = (values - mean).astype(BF16).astype(F32)
        power = jnp.sum(centered * centered, axis=1, keepdims=True) / L
        factor = 1.0 / (NCH * L * jnp.sqrt(power + 1e-06))
        row = jnp.sum(jnp.where(owner_row == owner_lane, factor, 0.0), axis=0, keepdims=True)
        factors_ref[c] = jnp.broadcast_to(row, (ROWS, own * LAGS))
        before = [jnp.zeros((LAGS, LANES), F32)] * own
        for k in range(wave_blocks + 1):
            if k < wave_blocks:
                turned = [
                    pltpu.roll(
                        jnp.broadcast_to(centered[t : t + 1, LANES * k : LANES * (k + 1)], (LAGS, LANES)),
                        0, 1, stride=1, stride_axis=0,
                    )
                    for t in range(own)
                ]
            else:
                turned = [jnp.zeros((LAGS, LANES), F32)] * own
            for g in range(groups):
                merged = jnp.concatenate(
                    [jnp.where(upper, turned[t], before[t]) for t in range(SUB * g, SUB * (g + 1))], axis=0
                )
                bands[c, LANES * k : LANES * (k + 1), LANES * g : LANES * (g + 1)] = merged.T.astype(BF16)
            before = turned

    @pl.when(early)
    def _():
        pl.semaphore_wait(late_sem, n - late_from)
        for d in range(late_from, n):
            send(d)

    for fetch in fetches[2:]:
        fetch.wait()
    width = counts_ref.shape[1]
    first_own = me * own

    def near(ref):
        found = ref[:, :LANES]
        for b in range(1, width // LANES):
            found = jnp.where(first_own // LANES == b, ref[:, LANES * b : LANES * (b + 1)], found)
        return found

    lists, counts, offsets = near(lists_ref), near(counts_ref), near(offsets_ref)
    station = lax.broadcasted_iota(jnp.int32, (n, LANES), 0)
    lane = lax.broadcasted_iota(jnp.int32, (n, LANES), 1)
    table = jnp.zeros((n, LANES), jnp.int32)
    for k in range(lists_ref.shape[0]):
        match = (lists[k : k + 1, :] == station) & (k < counts)
        table = table + jnp.where(match, offsets[k : k + 1, :] + 256, 0)
    here = lax.rem(first_own, LANES)
    for g in range(groups):
        for v in range(SUB):
            group = lax.bitwise_xor(lane // LAGS, v)
            code = jnp.take_along_axis(table, here + SUB * g + group, axis=1, mode="promise_in_bounds")
            sources[g, v] = LAGS * group + ((lane + code) & (LAGS - 1))
            if v == 0:
                lane_codes[g] = code

    def stage(sender):
        samples = slots[sender].astype(F32)
        for b in range(blocks):
            first_row = pl.multiple_of(sender * station_rows + ROWS * b, ROWS)
            staged[pl.ds(first_row, NCH), :] = samples[:, LANES * b : LANES * (b + 1)]

    lane = lax.broadcasted_iota(jnp.int32, (ROWS, LANES), 1)
    sub = lax.broadcasted_iota(jnp.int32, (ROWS, LANES), 0)
    inner = lane & (LAGS - 1)
    lane_group = lane // LAGS
    octets = n // ROWS
    out_parts = NTAU // LAGS
    out_blocks = NTAU // LANES
    total = [[[None] * SUB for _ in range(groups)] for _ in range(out_blocks)]

    for turn in range(octets):
        first = jnp.where(early, turn, octets - 1 - turn) * ROWS

        @pl.loop(0, ROWS)
        def receive(i):
            sender = first + i

            @pl.when(sender != me)
            def _():
                pltpu.make_async_remote_copy(
                    src_ref=slots.at[sender],
                    dst_ref=slots.at[sender],
                    send_sem=send_sem.at[sender],
                    recv_sem=recv_sem.at[sender],
                    device_id={"sta": sender},
                    device_id_type=MESH,
                ).wait_recv()

        for i in range(ROWS):
            stage(first + i)

        parts = [
            [staged[pl.ds(first * station_rows + ROWS * b + c, ROWS, stride=station_rows), :] for b in range(blocks)]
            for c in range(NCH)
        ]

        pieces = []
        for b in range(blocks):
            rows = [parts[c][b] for c in range(NCH)]
            for c in range(NCH):
                square = parts[c][b] * parts[c][b]
                high = square.astype(BF16).astype(F32)
                rows += [high, square - high]
            rows.append(rows[0])
            pieces.append(jnp.concatenate(rows, axis=0).astype(BF16))
        stacked = jnp.concatenate(
            [jnp.concatenate(pieces[b : b + wave_blocks + 1], axis=1) for b in range(lag_blocks)], axis=0
        )
        sums = jnp.dot(stacked, window_ref[...], preferred_element_type=F32)
        held = ROWS * (3 * NCH + 1)

        fitted = [[None] * groups for _ in range(parts_of_lags)]
        for c in range(NCH):
            shifted = [parts[c]]
            for j in range(1, SUB):
                rolled = [pltpu.roll(x, LANES - LAGS * j, 1) for x in parts[c]]
                stays = lane < LANES - LAGS * j
                shifted.append(
                    [jnp.where(stays, rolled[b], rolled[b + 1]) for b in range(blocks - 1)] + [rolled[-1]]
                )
            packed = [
                [jnp.concatenate([shifted[j][b], shifted[j + 1][b]], axis=0).astype(BF16) for b in range(blocks)]
                for j in range(0, SUB, 2)
            ]
            operand = jnp.concatenate(
                [
                    jnp.concatenate(packed[j][b : b + wave_blocks + 1], axis=1)
                    for b in range(lag_blocks)
                    for j in range(SUB // 2)
                ],
                axis=0,
            )
            products = jnp.dot(operand, bands[c], preferred_element_type=F32)
            for b in range(lag_blocks):
                base = held * b
                mean_one = sums[base + ROWS * c : base + ROWS * (c + 1)] / L
                at = base + ROWS * (NCH + 2 * c)
                mean_two = (sums[at : at + ROWS] + sums[at + ROWS : at + 2 * ROWS]) / L
                inverse = lax.rsqrt(mean_two - mean_one * mean_one + 1e-05)
                for j in range(SUB):
                    k = SUB * b + j
                    spread = jnp.take_along_axis(inverse, inner + LAGS * j, axis=1, mode="promise_in_bounds")
                    for g in range(groups):
                        lanes = slice(LANES * g, LANES * (g + 1))
                        term = products[ROWS * k : ROWS * (k + 1), lanes] * (spread * factors_ref[c, :, lanes])
                        fitted[k][g] = term if c == 0 else fitted[k][g] + term

        rows = pl.ds(pl.multiple_of(first, ROWS), ROWS)
        for g in range(groups):
            code = lane_codes[g, rows, :]
            far, half, member = (code & 64) != 0, (code & 32) != 0, code >= 256
            wraps = inner < (code & (LAGS - 1))
            one = [jnp.where(far, fitted[k + 2][g], fitted[k][g]) for k in range(out_parts + 2)]
            two = [jnp.where(half, one[k + 1], one[k]) for k in range(out_parts + 1)]
            picked = [
                jnp.where(member, jnp.where(wraps, two[k + 1], two[k]), 0.0) for k in range(out_parts)
            ]
            for b in range(out_blocks):
                mixed = picked[SUB * b : SUB * (b + 1)]
                for bit in (1, 2):
                    flipped = (lane_group & bit) != 0
                    mixed = [jnp.where(flipped, mixed[v ^ bit], mixed[v]) for v in range(SUB)]
                for v in range(SUB):
                    moved = jnp.take_along_axis(mixed[v], sources[g, v, rows, :], axis=1, mode="promise_in_bounds")
                    total[b][g][v] = moved if turn == 0 else total[b][g][v] + moved

    for b in range(out_blocks):
        level = [x for g in range(groups) for x in total[b][g]]
        distance = 1
        while distance < ROWS:
            low = (sub & distance) == 0
            if distance < SUB:
                low = low == ((lane_group & distance) == 0)
            level = [
                jnp.where(low, x, y) + pltpu.roll(jnp.where(low, y, x), distance, 0)
                for x, y in zip(level[::2], level[1::2])
            ]
            distance *= 2
        out_ref[:, LANES * b : LANES * (b + 1)] = level[0]

    @pl.loop(1, n)
    def sent(step):
        copy_to(lax.rem(me + step, n)).wait_send()


def body(n, data, templates, station_lists, counts, offsets):
    own, _, length = templates.shape
    operands = (data, jnp.transpose(templates, (1, 0, 2)), station_lists, counts[None, :], offsets)
    return pl.pallas_call(
        functools.partial(network_kernel, n),
        out_shape=jax.ShapeDtypeStruct((own, NTAU), F32),
        in_specs=[pl.BlockSpec(memory_space=pltpu.HBM)] * len(operands),
        out_specs=pl.BlockSpec(memory_space=pltpu.VMEM),
        scratch_shapes=[pltpu.VMEM(x.shape, x.dtype) for x in operands[1:]]
        + [
            pltpu.VMEM((n, *data.shape[1:]), data.dtype),
            pltpu.VMEM((n * ROWS * (data.shape[2] // LANES), LANES), F32),
            pltpu.VMEM((NCH, length + LANES, own * LAGS), BF16),
            pltpu.VMEM((NCH, ROWS, own * LAGS), F32),
            pltpu.VMEM((length + LANES, LANES), BF16),
            pltpu.VMEM((own // SUB, n, LANES), jnp.int32),
            pltpu.VMEM((own // SUB, SUB, n, LANES), jnp.int32),
            pltpu.SemaphoreType.DMA((len(operands),)),
            pltpu.SemaphoreType.DMA((n,)),
            pltpu.SemaphoreType.DMA((n,)),
            pltpu.SemaphoreType.REGULAR,
        ],
        compiler_params=pltpu.CompilerParams(
            collective_id=0, has_side_effects=True, vmem_limit_bytes=40 * 1024 * 1024
        ),
    )(*[pltpu.with_memory_space_constraint(x, pltpu.HBM) for x in operands])


def solution(mesh):
    placed = (P(("parts", "sta"), None, None), P("sta", None, None), P(), P(), P())
    return jax.shard_map(
        functools.partial(body, mesh.shape["sta"]), mesh=mesh, in_specs=placed,
        out_specs=P(("parts", "sta"), None), check_vma=False,
    )
```

time: 11.2 us -> 10.2 us (0.911)
  Pallas kernels: 10.4 us -> 9.35 us
    pallas_call x1, Pallas kernels: 10.4 us -> 9.35 us  [body(): pl.pallas_call(functools.partial(network_kernel, n), out_shape=jax.ShapeD...]
where the time goes in v1:
time: 10.2 us; the launch traced here: 9.96 us
  Pallas kernels  9.35 us (92%)
  local copies, waits for them, and re-layouts  0.6 us (6%)
    pallas_call x1, Pallas kernels, body(): pl.pallas_call(functools.partial(network_kernel, n), out_shape=jax.ShapeD...  9.35 us
    unnamed x1, local copies, waits for them, and re-layouts  0.6 us

profile of v1, /device:TPU:0, one launch (start us, length us, event | category | flops | bytes accessed | tf_op | source)
XLA Modules:
  0.0 10.0 jit_solution(12921566635529509931)
XLA Ops:
  0.0 9.4 %shard_map.55 = f32[8,256]{1,0:T(8,128)S(1)} custom-call(bf16[1,3,896]{2,1,0:T(4,128)(2,1)} %data_hbm.1, bf16[3,8,512]{2,1,0:T(8,128)(2,1)} %bitcast.2, s32[16,128]{1,0:T(8,128)} %lists_hbm.1, s32[1,128]{1,0:T(1,128)} %bitcast.3, s32[16,128]{1,0:T(8,128)} %offsets_hbm.1), custom_call_target="tpu_custom_call" | custom-call | tf_op jit(solution)/shard_map/pallas_call | solution.py:303
  9.4 0.6 %copy.7 = f32[8,256]{1,0:T(8,128)} copy(f32[8,256]{1,0:T(8,128)S(1)} %shard_map.55) | data formatting | bytes 16384

commit v2 on v1

--- a/solution.py
+++ b/solution.py
@@ -40,7 +40,6 @@
     blocks = samples_len // LANES
     lag_blocks = (samples_len - L) // LANES
     wave_blocks = L // LANES
-    depth = L + LANES
     own = templates_ref.shape[1]
     groups = own // SUB
     station_rows = ROWS * blocks
@@ -50,21 +49,23 @@
     early = me < late_from
     barrier = pltpu.get_barrier_semaphore()
 
-    def to_others(low, high, act):
-        for d in range(low, high):
-            pl.when(me != d)(functools.partial(act, d))
+    def others(low, high):
+        return [d + jnp.where(me <= d, 1, 0).astype(jnp.int32) for d in range(low, high - 1)]
 
     def greet(d):
-        pl.semaphore_signal(barrier, inc=1, device_id={"sta": jnp.int32(d)}, device_id_type=MESH)
-
-    def announce(d):
-        pl.semaphore_signal(late_sem, inc=1, device_id={"sta": jnp.int32(d)}, device_id_type=MESH)
-
-    to_others(late_from, n, greet)
+        pl.semaphore_signal(barrier, inc=1, device_id={"sta": d}, device_id_type=MESH)
 
     @pl.when(early)
     def _():
-        to_others(0, late_from, greet)
+        for d in range(late_from, n):
+            greet(jnp.int32(d))
+        for d in others(0, late_from):
+            greet(d)
+
+    @pl.when(jnp.logical_not(early))
+    def _():
+        for d in others(late_from, n):
+            greet(d)
 
     for fetch in fetches[1:]:
         fetch.start()
@@ -73,32 +74,32 @@
         return pltpu.make_async_remote_copy(
             src_ref=slots.at[me],
             dst_ref=slots.at[me],
-            send_sem=send_sem.at[target],
-            recv_sem=recv_sem.at[me],
+            send_sem=send_sem,
+            recv_sem=recv_sem.at[me // ROWS],
             device_id={"sta": target},
             device_id_type=MESH,
         )
 
-    def send(d):
-        copy_to(jnp.int32(d)).start()
-
     fetches[0].wait()
 
     @pl.when(early)
     def _():
         pl.semaphore_wait(barrier, late_from - 1)
-        to_others(0, late_from, send)
+        for d in others(0, late_from):
+            copy_to(d).start()
 
     @pl.when(jnp.logical_not(early))
     def _():
         pl.semaphore_wait(barrier, n - 1)
         for d in range(late_from):
-            announce(d)
-        to_others(0, n, send)
-
-    window_row = lax.broadcasted_iota(jnp.int32, (depth, LANES), 0)
-    window_lane = lax.broadcasted_iota(jnp.int32, (depth, LANES), 1)
-    window = ((window_row >= window_lane) & (window_row < window_lane + L)).astype(F32)
+            copy_to(jnp.int32(d)).start()
+            pl.semaphore_signal(late_sem, inc=1, device_id={"sta": jnp.int32(d)}, device_id_type=MESH)
+        for d in others(late_from, n):
+            copy_to(d).start()
+
+    window_row = lax.broadcasted_iota(jnp.int32, (2 * LANES, LANES), 0)
+    window_lane = lax.broadcasted_iota(jnp.int32, (2 * LANES, LANES), 1)
+    window = ((window_row >= window_lane) & (window_row < window_lane + LANES)).astype(F32)
     window_ref[...] = window.astype(BF16)
 
     fetches[1].wait()
@@ -138,7 +139,7 @@
     def _():
         pl.semaphore_wait(late_sem, n - late_from)
         for d in range(late_from, n):
-            send(d)
+            copy_to(jnp.int32(d)).start()
 
     for fetch in fetches[2:]:
         fetch.wait()
@@ -167,6 +168,10 @@
             if v == 0:
                 lane_codes[g] = code
 
+    def arrival(semaphore, count):
+        some = slots.at[pl.ds(0, count)]
+        return pltpu.make_async_copy(some, some, semaphore)
+
     def stage(sender):
         samples = slots[sender].astype(F32)
         for b in range(blocks):
@@ -185,21 +190,11 @@
     for turn in range(octets):
         first = jnp.where(early, turn, octets - 1 - turn) * ROWS
 
-        @pl.loop(0, ROWS)
-        def receive(i):
-            sender = first + i
-
-            @pl.when(sender != me)
-            def _():
-                pltpu.make_async_remote_copy(
-                    src_ref=slots.at[sender],
-                    dst_ref=slots.at[sender],
-                    send_sem=send_sem.at[sender],
-                    recv_sem=recv_sem.at[sender],
-                    device_id={"sta": sender},
-                    device_id_type=MESH,
-                ).wait_recv()
-
+        octet = first // ROWS
+        if turn == octets - 1:
+            arrival(send_sem, n - 1).wait()
+        pl.when(me // ROWS == octet)(arrival(recv_sem.at[octet], ROWS - 1).wait)
+        pl.when(me // ROWS != octet)(arrival(recv_sem.at[octet], ROWS).wait)
         for i in range(ROWS):
             stage(first + i)
 
@@ -208,17 +203,28 @@
             for c in range(NCH)
         ]
 
+        squares = [[x * x for x in parts[c]] for c in range(NCH)]
+        inside = [
+            [
+                [
+                    jnp.sum(functools.reduce(jnp.add, x[b + 1 : b + wave_blocks]), axis=1, keepdims=True)
+                    for x in (parts[c], squares[c])
+                ]
+                for b in range(lag_blocks)
+            ]
+            for c in range(NCH)
+        ]
         pieces = []
         for b in range(blocks):
             rows = [parts[c][b] for c in range(NCH)]
             for c in range(NCH):
-                square = parts[c][b] * parts[c][b]
+                square = squares[c][b]
                 high = square.astype(BF16).astype(F32)
                 rows += [high, square - high]
             rows.append(rows[0])
             pieces.append(jnp.concatenate(rows, axis=0).astype(BF16))
         stacked = jnp.concatenate(
-            [jnp.concatenate(pieces[b : b + wave_blocks + 1], axis=1) for b in range(lag_blocks)], axis=0
+            [jnp.concatenate([pieces[b], pieces[b + wave_blocks]], axis=1) for b in range(lag_blocks)], axis=0
         )
         sums = jnp.dot(stacked, window_ref[...], preferred_element_type=F32)
         held = ROWS * (3 * NCH + 1)
@@ -247,9 +253,10 @@
             products = jnp.dot(operand, bands[c], preferred_element_type=F32)
             for b in range(lag_blocks):
                 base = held * b
-                mean_one = sums[base + ROWS * c : base + ROWS * (c + 1)] / L
+                whole, whole_squares = inside[c][b]
+                mean_one = (sums[base + ROWS * c : base + ROWS * (c + 1)] + whole) / L
                 at = base + ROWS * (NCH + 2 * c)
-                mean_two = (sums[at : at + ROWS] + sums[at + ROWS : at + 2 * ROWS]) / L
+                mean_two = (sums[at : at + ROWS] + sums[at + ROWS : at + 2 * ROWS] + whole_squares) / L
                 inverse = lax.rsqrt(mean_two - mean_one * mean_one + 1e-05)
                 for j in range(SUB):
                     k = SUB * b + j
@@ -291,10 +298,6 @@
             ]
             distance *= 2
         out_ref[:, LANES * b : LANES * (b + 1)] = level[0]
-
-    @pl.loop(1, n)
-    def sent(step):
-        copy_to(lax.rem(me + step, n)).wait_send()
 
 
 def body(n, data, templates, station_lists, counts, offsets):
@@ -311,12 +314,12 @@
             pltpu.VMEM((n * ROWS * (data.shape[2] // LANES), LANES), F32),
             pltpu.VMEM((NCH, length + LANES, own * LAGS), BF16),
             pltpu.VMEM((NCH, ROWS, own * LAGS), F32),
-            pltpu.VMEM((length + LANES, LANES), BF16),
+            pltpu.VMEM((2 * LANES, LANES), BF16),
             pltpu.VMEM((own // SUB, n, LANES), jnp.int32),
             pltpu.VMEM((own // SUB, SUB, n, LANES), jnp.int32),
             pltpu.SemaphoreType.DMA((len(operands),)),
-            pltpu.SemaphoreType.DMA((n,)),
-            pltpu.SemaphoreType.DMA((n,)),
+            pltpu.SemaphoreType.DMA,
+            pltpu.SemaphoreType.DMA((n // ROWS,)),
             pltpu.SemaphoreType.REGULAR,
         ],
         compiler_params=pltpu.CompilerParams(

time: 10.2 us -> 9.72 us (0.953)
  Pallas kernels: 9.35 us -> 8.92 us
    pallas_call x1, Pallas kernels: 9.35 us -> 8.92 us  [body(): pl.pallas_call(functools.partial(network_kernel, n), out_shape=jax.ShapeD...]
where the time goes in v2:
time: 9.72 us; the launch traced here: 9.53 us
  Pallas kernels  8.92 us (92%)
  local copies, waits for them, and re-layouts  0.6 us (6%)
    pallas_call x1, Pallas kernels, body(): pl.pallas_call(functools.partial(network_kernel, n), out_shape=jax.ShapeD...  8.92 us
    unnamed x1, local copies, waits for them, and re-layouts  0.6 us

profile of v2, /device:TPU:0, one launch (start us, length us, event | category | flops | bytes accessed | tf_op | source)
XLA Modules:
  0.0 9.5 jit_solution(6114536331369319780)
XLA Ops:
  0.0 8.9 %shard_map.55 = f32[8,256]{1,0:T(8,128)S(1)} custom-call(bf16[1,3,896]{2,1,0:T(4,128)(2,1)} %data_hbm.1, bf16[3,8,512]{2,1,0:T(8,128)(2,1)} %bitcast.2, s32[16,128]{1,0:T(8,128)} %lists_hbm.1, s32[1,128]{1,0:T(1,128)} %bitcast.3, s32[16,128]{1,0:T(8,128)} %offsets_hbm.1), custom_call_target="tpu_custom_call" | custom-call | tf_op jit(solution)/shard_map/pallas_call | solution.py:306
  8.9 0.6 %copy.7 = f32[8,256]{1,0:T(8,128)} copy(f32[8,256]{1,0:T(8,128)S(1)} %shard_map.55) | data formatting | bytes 16384

commit v3 on v2

--- a/solution.py
+++ b/solution.py
@@ -23,7 +23,7 @@
     n, data_hbm, templates_hbm, lists_hbm, counts_hbm, offsets_hbm, out_ref,
     templates_ref, lists_ref, counts_ref, offsets_ref,
     slots, staged, bands, factors_ref, window_ref, lane_codes, sources,
-    fetch_sem, send_sem, recv_sem, late_sem,
+    fetch_sem, send_sem, recv_sem, joined, complete,
 ):
     me = lax.axis_index("sta")
     fetches = [
@@ -45,34 +45,38 @@
     station_rows = ROWS * blocks
     parts_of_lags = lag_blocks * SUB
 
-    late_from = n - n // 4
+    gap = n // 4
+    late_from = n - gap
+    roots = 2
     early = me < late_from
     barrier = pltpu.get_barrier_semaphore()
 
     def others(low, high):
         return [d + jnp.where(me <= d, 1, 0).astype(jnp.int32) for d in range(low, high - 1)]
 
-    def greet(d):
-        pl.semaphore_signal(barrier, inc=1, device_id={"sta": d}, device_id_type=MESH)
+    def tell(semaphore, d):
+        pl.semaphore_signal(semaphore, inc=1, device_id={"sta": d}, device_id_type=MESH)
+
+    direct = late_from + gap // 2
+
+    @pl.when(me < roots)
+    def _():
+        for d in reversed(range(direct, n)):
+            tell(barrier, jnp.int32(d))
 
     @pl.when(early)
     def _():
-        for d in range(late_from, n):
-            greet(jnp.int32(d))
+        for d in range(late_from, direct):
+            tell(barrier, jnp.int32(d))
         for d in others(0, late_from):
-            greet(d)
-
-    @pl.when(jnp.logical_not(early))
-    def _():
-        for d in others(late_from, n):
-            greet(d)
+            tell(barrier, d)
 
     for fetch in fetches[1:]:
         fetch.start()
 
-    def copy_to(target):
+    def copy_to(target, source=slots.at[me]):
         return pltpu.make_async_remote_copy(
-            src_ref=slots.at[me],
+            src_ref=source,
             dst_ref=slots.at[me],
             send_sem=send_sem,
             recv_sem=recv_sem.at[me // ROWS],
@@ -80,22 +84,39 @@
             device_id_type=MESH,
         )
 
-    fetches[0].wait()
-
     @pl.when(early)
     def _():
+        fetches[0].wait()
         pl.semaphore_wait(barrier, late_from - 1)
+
+        @pl.when((me + gap >= direct) & (me + gap < n))
+        def _():
+            tell(barrier, me + gap)
+
         for d in others(0, late_from):
             copy_to(d).start()
 
     @pl.when(jnp.logical_not(early))
     def _():
-        pl.semaphore_wait(barrier, n - 1)
-        for d in range(late_from):
-            copy_to(jnp.int32(d)).start()
-            pl.semaphore_signal(late_sem, inc=1, device_id={"sta": jnp.int32(d)}, device_id_type=MESH)
-        for d in others(late_from, n):
-            copy_to(d).start()
+        @pl.when(me < direct)
+        def _():
+            fetches[0].wait()
+            pl.semaphore_wait(barrier, late_from)
+            for d in range(late_from):
+                copy_to(jnp.int32(d)).start()
+                tell(joined, jnp.int32(d))
+
+        @pl.when(me >= direct)
+        def _():
+            pl.semaphore_wait(barrier, roots)
+            for d in range(roots):
+                copy_to(jnp.int32(d), data_hbm.at[0]).start()
+                tell(joined, jnp.int32(d))
+            fetches[0].wait()
+            pl.semaphore_wait(barrier, 1)
+            for d in range(roots, late_from):
+                tell(joined, jnp.int32(d))
+                copy_to(jnp.int32(d)).start()
 
     window_row = lax.broadcasted_iota(jnp.int32, (2 * LANES, LANES), 0)
     window_lane = lax.broadcasted_iota(jnp.int32, (2 * LANES, LANES), 1)
@@ -137,9 +158,20 @@
 
     @pl.when(early)
     def _():
-        pl.semaphore_wait(late_sem, n - late_from)
+        pl.semaphore_wait(joined, n - late_from)
+
+        @pl.when(me >= late_from - gap)
+        def _():
+            tell(complete, me + gap)
+
         for d in range(late_from, n):
             copy_to(jnp.int32(d)).start()
+
+    @pl.when(jnp.logical_not(early))
+    def _():
+        pl.semaphore_wait(complete, 1)
+        for d in others(late_from, n):
+            copy_to(d).start()
 
     for fetch in fetches[2:]:
         fetch.wait()
@@ -321,6 +353,7 @@
             pltpu.SemaphoreType.DMA,
             pltpu.SemaphoreType.DMA((n // ROWS,)),
             pltpu.SemaphoreType.REGULAR,
+            pltpu.SemaphoreType.REGULAR,
         ],
         compiler_params=pltpu.CompilerParams(
             collective_id=0, has_side_effects=True, vmem_limit_bytes=40 * 1024 * 1024

time: 9.72 us -> 9.56 us (0.984)
  Pallas kernels: 8.92 us -> 8.76 us
    pallas_call x1, Pallas kernels: 8.92 us -> 8.76 us  [body(): pl.pallas_call(functools.partial(network_kernel, n), out_shape=jax.ShapeD...]
where the time goes in v3:
time: 9.56 us; the launch traced here: 9.37 us
  Pallas kernels  8.76 us (92%)
  local copies, waits for them, and re-layouts  0.6 us (6%)
    pallas_call x1, Pallas kernels, body(): pl.pallas_call(functools.partial(network_kernel, n), out_shape=jax.ShapeD...  8.76 us
    unnamed x1, local copies, waits for them, and re-layouts  0.6 us

profile of v3, /device:TPU:0, one launch (start us, length us, event | category | flops | bytes accessed | tf_op | source)
XLA Modules:
  0.0 9.4 jit_solution(18195883564199266363)
XLA Ops:
  0.0 8.8 %shard_map.55 = f32[8,256]{1,0:T(8,128)S(1)} custom-call(bf16[1,3,896]{2,1,0:T(4,128)(2,1)} %data_hbm.1, bf16[3,8,512]{2,1,0:T(8,128)(2,1)} %bitcast.2, s32[16,128]{1,0:T(8,128)} %lists_hbm.1, s32[1,128]{1,0:T(1,128)} %bitcast.3, s32[16,128]{1,0:T(8,128)} %offsets_hbm.1), custom_call_target="tpu_custom_call" | custom-call | tf_op jit(solution)/shard_map/pallas_call | solution.py:338
  8.8 0.6 %copy.7 = f32[8,256]{1,0:T(8,128)} copy(f32[8,256]{1,0:T(8,128)S(1)} %shard_map.55) | data formatting | bytes 16384

commit v4 on v3

--- a/solution.py
+++ b/solution.py
@@ -22,7 +22,7 @@
 def network_kernel(
     n, data_hbm, templates_hbm, lists_hbm, counts_hbm, offsets_hbm, out_ref,
     templates_ref, lists_ref, counts_ref, offsets_ref,
-    slots, staged, bands, factors_ref, window_ref, lane_codes, sources,
+    slots, staged, bands, factors_ref, window_ref, lane_codes, sources, totals,
     fetch_sem, send_sem, recv_sem, joined, complete,
 ):
     me = lax.axis_index("sta")
@@ -35,7 +35,6 @@
             ]
         )
     ]
-    fetches[0].start()
     samples_len = data_hbm.shape[2]
     blocks = samples_len // LANES
     lag_blocks = (samples_len - L) // LANES
@@ -58,21 +57,12 @@
         pl.semaphore_signal(semaphore, inc=1, device_id={"sta": d}, device_id_type=MESH)
 
     direct = late_from + gap // 2
+    far_from = late_from - gap
 
     @pl.when(me < roots)
     def _():
         for d in reversed(range(direct, n)):
             tell(barrier, jnp.int32(d))
-
-    @pl.when(early)
-    def _():
-        for d in range(late_from, direct):
-            tell(barrier, jnp.int32(d))
-        for d in others(0, late_from):
-            tell(barrier, d)
-
-    for fetch in fetches[1:]:
-        fetch.start()
 
     def copy_to(target, source=slots.at[me]):
         return pltpu.make_async_remote_copy(
@@ -84,6 +74,25 @@
             device_id_type=MESH,
         )
 
+    @pl.when(me >= direct)
+    def _():
+        pl.semaphore_wait(barrier, roots)
+        for d in range(roots):
+            copy_to(jnp.int32(d), data_hbm.at[0]).start()
+            tell(joined.at[1], jnp.int32(d))
+
+    fetches[0].start()
+
+    @pl.when(early)
+    def _():
+        for d in range(late_from, direct):
+            tell(barrier, jnp.int32(d))
+        for d in others(0, late_from):
+            tell(barrier, d)
+
+    for fetch in fetches[1:]:
+        fetch.start()
+
     @pl.when(early)
     def _():
         fetches[0].wait()
@@ -93,8 +102,17 @@
         def _():
             tell(barrier, me + gap)
 
-        for d in others(0, late_from):
-            copy_to(d).start()
+        @pl.when(me < far_from)
+        def _():
+            for d in others(0, late_from):
+                copy_to(d).start()
+
+        @pl.when(me >= far_from)
+        def _():
+            for d in range(roots):
+                copy_to(jnp.int32(d)).start()
+            for d in others(far_from, late_from):
+                copy_to(d).start()
 
     @pl.when(jnp.logical_not(early))
     def _():
@@ -103,19 +121,16 @@
             fetches[0].wait()
             pl.semaphore_wait(barrier, late_from)
             for d in range(late_from):
-                copy_to(jnp.int32(d)).start()
-                tell(joined, jnp.int32(d))
+                tell(joined.at[0], jnp.int32(d))
+                if d < roots:
+                    copy_to(jnp.int32(d)).start()
 
         @pl.when(me >= direct)
         def _():
-            pl.semaphore_wait(barrier, roots)
-            for d in range(roots):
-                copy_to(jnp.int32(d), data_hbm.at[0]).start()
-                tell(joined, jnp.int32(d))
             fetches[0].wait()
             pl.semaphore_wait(barrier, 1)
             for d in range(roots, late_from):
-                tell(joined, jnp.int32(d))
+                tell(joined.at[1], jnp.int32(d))
                 copy_to(jnp.int32(d)).start()
 
     window_row = lax.broadcasted_iota(jnp.int32, (2 * LANES, LANES), 0)
@@ -158,17 +173,33 @@
 
     @pl.when(early)
     def _():
-        pl.semaphore_wait(joined, n - late_from)
-
-        @pl.when(me >= late_from - gap)
+        @pl.when(me >= far_from)
+        def _():
+            for d in range(roots, far_from):
+                copy_to(jnp.int32(d)).start()
+
+        pl.semaphore_wait(joined.at[0], direct - late_from)
+        for d in reversed(range(late_from, direct)):
+            copy_to(jnp.int32(d)).start()
+
+    @pl.when(early)
+    def _():
+        pl.semaphore_wait(joined.at[1], n - direct)
+
+        @pl.when(me >= far_from)
         def _():
             tell(complete, me + gap)
 
-        for d in range(late_from, n):
+        for d in range(direct, n):
             copy_to(jnp.int32(d)).start()
 
     @pl.when(jnp.logical_not(early))
     def _():
+        @pl.when(me < direct)
+        def _():
+            for d in range(roots, late_from):
+                copy_to(jnp.int32(d)).start()
+
         pl.semaphore_wait(complete, 1)
         for d in others(late_from, n):
             copy_to(d).start()
@@ -217,14 +248,22 @@
     octets = n // ROWS
     out_parts = NTAU // LAGS
     out_blocks = NTAU // LANES
-    total = [[[None] * SUB for _ in range(groups)] for _ in range(out_blocks)]
-
-    for turn in range(octets):
+
+    totals[...] = jnp.zeros_like(totals)
+
+    @pl.loop(0, octets)
+    def work_off(turn):
         first = jnp.where(early, turn, octets - 1 - turn) * ROWS
 
         octet = first // ROWS
-        if turn == octets - 1:
-            arrival(send_sem, n - 1).wait()
+        here_rows = pl.ds(pl.multiple_of(first, ROWS), ROWS)
+        masked = [
+            [
+                jnp.where(lane_codes[g, here_rows, :] >= 256, factors_ref[c, :, LANES * g : LANES * (g + 1)], 0.0)
+                for g in range(groups)
+            ]
+            for c in range(NCH)
+        ]
         pl.when(me // ROWS == octet)(arrival(recv_sem.at[octet], ROWS - 1).wait)
         pl.when(me // ROWS != octet)(arrival(recv_sem.at[octet], ROWS).wait)
         for i in range(ROWS):
@@ -261,6 +300,16 @@
         sums = jnp.dot(stacked, window_ref[...], preferred_element_type=F32)
         held = ROWS * (3 * NCH + 1)
 
+        inverses = [[] for _ in range(NCH)]
+        for c in range(NCH):
+            for b in range(lag_blocks):
+                base = held * b
+                whole, whole_squares = inside[c][b]
+                mean_one = (sums[base + ROWS * c : base + ROWS * (c + 1)] + whole) / L
+                at = base + ROWS * (NCH + 2 * c)
+                mean_two = (sums[at : at + ROWS] + sums[at + ROWS : at + 2 * ROWS] + whole_squares) / L
+                inverses[c].append(lax.rsqrt(mean_two - mean_one * mean_one + 1e-05))
+
         fitted = [[None] * groups for _ in range(parts_of_lags)]
         for c in range(NCH):
             shifted = [parts[c]]
@@ -284,41 +333,35 @@
             )
             products = jnp.dot(operand, bands[c], preferred_element_type=F32)
             for b in range(lag_blocks):
-                base = held * b
-                whole, whole_squares = inside[c][b]
-                mean_one = (sums[base + ROWS * c : base + ROWS * (c + 1)] + whole) / L
-                at = base + ROWS * (NCH + 2 * c)
-                mean_two = (sums[at : at + ROWS] + sums[at + ROWS : at + 2 * ROWS] + whole_squares) / L
-                inverse = lax.rsqrt(mean_two - mean_one * mean_one + 1e-05)
+                inverse = inverses[c][b]
                 for j in range(SUB):
                     k = SUB * b + j
                     spread = jnp.take_along_axis(inverse, inner + LAGS * j, axis=1, mode="promise_in_bounds")
                     for g in range(groups):
                         lanes = slice(LANES * g, LANES * (g + 1))
-                        term = products[ROWS * k : ROWS * (k + 1), lanes] * (spread * factors_ref[c, :, lanes])
+                        term = products[ROWS * k : ROWS * (k + 1), lanes] * (spread * masked[c][g])
                         fitted[k][g] = term if c == 0 else fitted[k][g] + term
 
-        rows = pl.ds(pl.multiple_of(first, ROWS), ROWS)
         for g in range(groups):
-            code = lane_codes[g, rows, :]
-            far, half, member = (code & 64) != 0, (code & 32) != 0, code >= 256
+            code = lane_codes[g, here_rows, :]
+            far, half = (code & 64) != 0, (code & 32) != 0
             wraps = inner < (code & (LAGS - 1))
             one = [jnp.where(far, fitted[k + 2][g], fitted[k][g]) for k in range(out_parts + 2)]
             two = [jnp.where(half, one[k + 1], one[k]) for k in range(out_parts + 1)]
-            picked = [
-                jnp.where(member, jnp.where(wraps, two[k + 1], two[k]), 0.0) for k in range(out_parts)
-            ]
+            picked = [jnp.where(wraps, two[k + 1], two[k]) for k in range(out_parts)]
             for b in range(out_blocks):
                 mixed = picked[SUB * b : SUB * (b + 1)]
                 for bit in (1, 2):
                     flipped = (lane_group & bit) != 0
                     mixed = [jnp.where(flipped, mixed[v ^ bit], mixed[v]) for v in range(SUB)]
                 for v in range(SUB):
-                    moved = jnp.take_along_axis(mixed[v], sources[g, v, rows, :], axis=1, mode="promise_in_bounds")
-                    total[b][g][v] = moved if turn == 0 else total[b][g][v] + moved
+                    moved = jnp.take_along_axis(mixed[v], sources[g, v, here_rows, :], axis=1, mode="promise_in_bounds")
+                    totals[b, g, v] += moved
+
+    arrival(send_sem, n - 1).wait()
 
     for b in range(out_blocks):
-        level = [x for g in range(groups) for x in total[b][g]]
+        level = [totals[b, g, v] for g in range(groups) for v in range(SUB)]
         distance = 1
         while distance < ROWS:
             low = (sub & distance) == 0
@@ -349,10 +392,11 @@
             pltpu.VMEM((2 * LANES, LANES), BF16),
             pltpu.VMEM((own // SUB, n, LANES), jnp.int32),
             pltpu.VMEM((own // SUB, SUB, n, LANES), jnp.int32),
+            pltpu.VMEM((NTAU // LANES, own // SUB, SUB, ROWS, LANES), F32),
             pltpu.SemaphoreType.DMA((len(operands),)),
             pltpu.SemaphoreType.DMA,
             pltpu.SemaphoreType.DMA((n // ROWS,)),
-            pltpu.SemaphoreType.REGULAR,
+            pltpu.SemaphoreType.REGULAR((2,)),
             pltpu.SemaphoreType.REGULAR,
         ],
         compiler_params=pltpu.CompilerParams(

time: 9.56 us -> 9.46 us (0.990)
  Pallas kernels: 8.76 us -> 8.66 us
    pallas_call x1, Pallas kernels: 8.76 us -> 8.66 us  [body(): pl.pallas_call(functools.partial(network_kernel, n), out_shape=jax.ShapeD...]
where the time goes in v4:
time: 9.46 us; the launch traced here: 9.27 us
  Pallas kernels  8.66 us (92%)
  local copies, waits for them, and re-layouts  0.6 us (6%)
    pallas_call x1, Pallas kernels, body(): pl.pallas_call(functools.partial(network_kernel, n), out_shape=jax.ShapeD...  8.66 us
    unnamed x1, local copies, waits for them, and re-layouts  0.6 us

profile of v4, /device:TPU:0, one launch (start us, length us, event | category | flops | bytes accessed | tf_op | source)
XLA Modules:
  0.0 9.3 jit_solution(18364164735644484351)
XLA Ops:
  0.0 8.7 %shard_map.55 = f32[8,256]{1,0:T(8,128)S(1)} custom-call(bf16[1,3,896]{2,1,0:T(4,128)(2,1)} %data_hbm.1, bf16[3,8,512]{2,1,0:T(8,128)(2,1)} %bitcast.2, s32[16,128]{1,0:T(8,128)} %lists_hbm.1, s32[1,128]{1,0:T(1,128)} %bitcast.3, s32[16,128]{1,0:T(8,128)} %offsets_hbm.1), custom_call_target="tpu_custom_call" | custom-call | tf_op jit(solution)/shard_map/pallas_call | solution.py:381
  8.7 0.6 %copy.7 = f32[8,256]{1,0:T(8,128)} copy(f32[8,256]{1,0:T(8,128)S(1)} %shard_map.55) | data formatting | bytes 16384

commit v5 on v4

--- a/solution.py
+++ b/solution.py
@@ -131,7 +131,6 @@
             pl.semaphore_wait(barrier, 1)
             for d in range(roots, late_from):
                 tell(joined.at[1], jnp.int32(d))
-                copy_to(jnp.int32(d)).start()
 
     window_row = lax.broadcasted_iota(jnp.int32, (2 * LANES, LANES), 0)
     window_lane = lax.broadcasted_iota(jnp.int32, (2 * LANES, LANES), 1)
@@ -195,10 +194,8 @@
 
     @pl.when(jnp.logical_not(early))
     def _():
-        @pl.when(me < direct)
-        def _():
-            for d in range(roots, late_from):
-                copy_to(jnp.int32(d)).start()
+        for d in range(roots, late_from):
+            copy_to(jnp.int32(d)).start()
 
         pl.semaphore_wait(complete, 1)
         for d in others(late_from, n):
@@ -386,7 +383,7 @@
         scratch_shapes=[pltpu.VMEM(x.shape, x.dtype) for x in operands[1:]]
         + [
             pltpu.VMEM((n, *data.shape[1:]), data.dtype),
-            pltpu.VMEM((n * ROWS * (data.shape[2] // LANES), LANES), F32),
+            pltpu.VMEM(((n + 1) * ROWS * (data.shape[2] // LANES), LANES), F32),
             pltpu.VMEM((NCH, length + LANES, own * LAGS), BF16),
             pltpu.VMEM((NCH, ROWS, own * LAGS), F32),
             pltpu.VMEM((2 * LANES, LANES), BF16),

time: 9.46 us -> 9.46 us (level)
  no operation moved by 1% of the time
where the time goes in v5:
time: 9.46 us; the launch traced here: 9.27 us
  Pallas kernels  8.66 us (92%)
  local copies, waits for them, and re-layouts  0.6 us (6%)
    pallas_call x1, Pallas kernels, body(): pl.pallas_call(functools.partial(network_kernel, n), out_shape=jax.ShapeD...  8.66 us
    unnamed x1, local copies, waits for them, and re-layouts  0.6 us

profile of v5, /device:TPU:0, one launch (start us, length us, event | category | flops | bytes accessed | tf_op | source)
XLA Modules:
  0.0 9.3 jit_solution(7544389780763066303)
XLA Ops:
  0.0 8.7 %shard_map.55 = f32[8,256]{1,0:T(8,128)S(1)} custom-call(bf16[1,3,896]{2,1,0:T(4,128)(2,1)} %data_hbm.1, bf16[3,8,512]{2,1,0:T(8,128)(2,1)} %bitcast.2, s32[16,128]{1,0:T(8,128)} %lists_hbm.1, s32[1,128]{1,0:T(1,128)} %bitcast.3, s32[16,128]{1,0:T(8,128)} %offsets_hbm.1), custom_call_target="tpu_custom_call" | custom-call | tf_op jit(solution)/shard_map/pallas_call | solution.py:378
  8.7 0.6 %copy.7 = f32[8,256]{1,0:T(8,128)} copy(f32[8,256]{1,0:T(8,128)S(1)} %shard_map.55) | data formatting | bytes 16384

commit v6 on v4

--- a/solution.py
+++ b/solution.py
@@ -251,8 +251,7 @@
 
     totals[...] = jnp.zeros_like(totals)
 
-    @pl.loop(0, octets)
-    def work_off(turn):
+    for turn in range(octets):
         first = jnp.where(early, turn, octets - 1 - turn) * ROWS
 
         octet = first // ROWS
@@ -386,7 +385,7 @@
         scratch_shapes=[pltpu.VMEM(x.shape, x.dtype) for x in operands[1:]]
         + [
             pltpu.VMEM((n, *data.shape[1:]), data.dtype),
-            pltpu.VMEM((n * ROWS * (data.shape[2] // LANES), LANES), F32),
+            pltpu.VMEM(((n + 1) * ROWS * (data.shape[2] // LANES), LANES), F32),
             pltpu.VMEM((NCH, length + LANES, own * LAGS), BF16),
             pltpu.VMEM((NCH, ROWS, own * LAGS), F32),
             pltpu.VMEM((2 * LANES, LANES), BF16),

time: 9.46 us -> 9.47 us (level)
  no operation moved by 1% of the time
where the time goes in v6:
time: 9.47 us; the launch traced here: 9.28 us
  Pallas kernels  8.67 us (92%)
  local copies, waits for them, and re-layouts  0.6 us (6%)
    pallas_call x1, Pallas kernels, body(): pl.pallas_call(functools.partial(network_kernel, n), out_shape=jax.ShapeD...  8.67 us
    unnamed x1, local copies, waits for them, and re-layouts  0.6 us

profile of v6, /device:TPU:0, one launch (start us, length us, event | category | flops | bytes accessed | tf_op | source)
XLA Modules:
  0.0 9.3 jit_solution(897572459871489257)
XLA Ops:
  0.0 8.7 %shard_map.55 = f32[8,256]{1,0:T(8,128)S(1)} custom-call(bf16[1,3,896]{2,1,0:T(4,128)(2,1)} %data_hbm.1, bf16[3,8,512]{2,1,0:T(8,128)(2,1)} %bitcast.2, s32[16,128]{1,0:T(8,128)} %lists_hbm.1, s32[1,128]{1,0:T(1,128)} %bitcast.3, s32[16,128]{1,0:T(8,128)} %offsets_hbm.1), custom_call_target="tpu_custom_call" | custom-call | tf_op jit(solution)/shard_map/pallas_call | solution.py:380
  8.7 0.6 %copy.7 = f32[8,256]{1,0:T(8,128)} copy(f32[8,256]{1,0:T(8,128)S(1)} %shard_map.55) | data formatting | bytes 16384

commit v7 on v4

--- a/solution.py
+++ b/solution.py
@@ -386,7 +386,7 @@
         scratch_shapes=[pltpu.VMEM(x.shape, x.dtype) for x in operands[1:]]
         + [
             pltpu.VMEM((n, *data.shape[1:]), data.dtype),
-            pltpu.VMEM((n * ROWS * (data.shape[2] // LANES), LANES), F32),
+            pltpu.VMEM(((n + 1) * ROWS * (data.shape[2] // LANES), LANES), F32),
             pltpu.VMEM((NCH, length + LANES, own * LAGS), BF16),
             pltpu.VMEM((NCH, ROWS, own * LAGS), F32),
             pltpu.VMEM((2 * LANES, LANES), BF16),

time: 9.46 us -> 9.46 us (level)
  no operation moved by 1% of the time
where the time goes in v7:
time: 9.46 us; the launch traced here: 9.27 us
  Pallas kernels  8.66 us (92%)
  local copies, waits for them, and re-layouts  0.6 us (6%)
    pallas_call x1, Pallas kernels, body(): pl.pallas_call(functools.partial(network_kernel, n), out_shape=jax.ShapeD...  8.66 us
    unnamed x1, local copies, waits for them, and re-layouts  0.6 us

profile of v7, /device:TPU:0, one launch (start us, length us, event | category | flops | bytes accessed | tf_op | source)
XLA Modules:
  0.0 9.3 jit_solution(8431220338083195816)
XLA Ops:
  0.0 8.7 %shard_map.55 = f32[8,256]{1,0:T(8,128)S(1)} custom-call(bf16[1,3,896]{2,1,0:T(4,128)(2,1)} %data_hbm.1, bf16[3,8,512]{2,1,0:T(8,128)(2,1)} %bitcast.2, s32[16,128]{1,0:T(8,128)} %lists_hbm.1, s32[1,128]{1,0:T(1,128)} %bitcast.3, s32[16,128]{1,0:T(8,128)} %offsets_hbm.1), custom_call_target="tpu_custom_call" | custom-call | tf_op jit(solution)/shard_map/pallas_call | solution.py:381
  8.7 0.6 %copy.7 = f32[8,256]{1,0:T(8,128)} copy(f32[8,256]{1,0:T(8,128)S(1)} %shard_map.55) | data formatting | bytes 16384
